TPU v7x, 32 devices: a whole 2x2x4 slice. The times are simulated.
32 devices in a mesh: rcv: 8 (over y, x, core), win: 4 (over z).
Axes of the slice: x: 2, y: 2, z: 4, core: 2. Of those that a mesh axis runs over, the one named last changes fastest.
Arguments:
- traces: bfloat16 [4096, 4, 6144], P('rcv', 'win'), may hold values from -6 to 6
- sources: int32 [8, 4], replicated, may hold values from 0 to 4095
- offsets: int32 [4], P('win'), may hold values from 0 to 44
Outputs:
- stacks: float32 [32, 101, 4096], P('win', None, 'rcv')
All inputs are finite; a program needn't handle non-finite values.
Results may differ from a plain program's by a relative error of at most 0.0003.
Values may be sent and summed in bfloat16 or wider, within the bound.
A program may use at most 192 MiB of HBM per device.

v0:
```python
import math

import jax
import jax.numpy as jnp
from jax import lax
from jax.sharding import PartitionSpec as P

SAMPLES = 6000
HALF = 50
LAGS = 101


def lag_matrix(record, start_at):
    span_len = record.shape[-1]
    positions = jnp.arange(span_len, dtype=jnp.int32)
    inside = (positions >= start_at + HALF) & (positions < start_at + HALF + SAMPLES)
    masked = jnp.where(inside[None, :], record, jnp.zeros_like(record))
    padded = jnp.pad(masked, ((0, 0), (LAGS, LAGS)))
    rows = []
    for lag in range(LAGS):
        begin = LAGS + HALF - lag
        rows.append(padded[:, begin : begin + span_len])
    return jnp.stack(rows, axis=1)


def shards(traces, sources, offsets):
    ch_dev = traces.shape[0]
    win_dev = traces.shape[1]
    step_count = sources.shape[0]
    win_count = lax.axis_size("win")
    first_row = lax.axis_index("rcv") * ch_dev
    window_total = win_dev * win_count
    norm_scale = 1.0 / math.sqrt(SAMPLES * window_total)
    channel_ids = jnp.arange(ch_dev, dtype=jnp.int32)
    results = []
    for step in range(step_count):
        select = (
            lax.dynamic_index_in_dim(sources, step, 0, keepdims=False)[:, None] - first_row
            == channel_ids[None, :]
        ).astype(traces.dtype)
        source_rows = lax.psum(
            jnp.einsum("kc,cwt->kwt", select, traces, preferred_element_type=jnp.float32).astype(
                jnp.bfloat16
            ),
            "rcv",
        )
        summed = jnp.zeros((source_rows.shape[0], LAGS, ch_dev), jnp.float32)
        shifted = lag_matrix(source_rows[:, 0, :], offsets[0])
        summed = summed + jnp.einsum(
            "kju,cu->kjc", shifted, traces[:, 0, :], preferred_element_type=jnp.float32
        )
        results.append(summed * norm_scale)
    stacked = jnp.concatenate(results, axis=0)
    return lax.psum_scatter(stacked, "win", scatter_dimension=0, tiled=True)


def solution(mesh):
    in_specs = (P("rcv", "win", None), P(), P("win"))
    out_specs = P("win", None, "rcv")
    return jax.shard_map(shards, mesh=mesh, in_specs=in_specs, out_specs=out_specs, check_vma=False)
```

profile of v0, /device:TPU:8, one launch (start us, length us, event | category | flops | bytes accessed | tf_op | source)
XLA Modules:
  0.0 759.2 jit_solution(12059561859957987986)
XLA Ops:
  6.5 1.3 subtract_reduce_fusion
  7.8 4.7 fusion.7
  12.5 1.6 fusion.5
  14.0 1.6 fusion.4
  15.6 1.6 fusion.3
  17.2 1.6 fusion.2
  18.8 1.6 fusion.1
  20.4 1.6 fusion
  22.0 1.6 fusion.6
  24.4 56.1 %all-reduce.11.cloned.1.call-done = (bf16[4,1,6144]{2,0,1:T(4,128)(2,1)}, bf16[4,1,6144]{2,0,1:T(4,128)(2,1)}, bf16[4,1,6144]{2,0,1:T(4,128)(2,1)}, bf16[4,1,614...) async-done(((bf16[4,1,6144]{2,0,1:T(4,128)(2,1)}, ...) | async-done | bytes 393232 | tf_op jit(solution)/shard_map/psum | solution.py:41
  80.5 1.2 bitcast_select_fusion
  92.4 0.7 constant_dynamic-update-slice_fusion.792
  121.7 0.7 constant_dynamic-update-slice_fusion.195
  123.1 0.7 constant_dynamic-update-slice_fusion.193
  166.7 0.7 constant_dynamic-update-slice_fusion.283
  186.6 0.7 constant_dynamic-update-slice_fusion.255
  212.4 0.9 constant_dynamic-update-slice_fusion.370
  256.8 0.7 constant_dynamic-update-slice_fusion.459
  257.5 0.7 constant_dynamic-update-slice_fusion.458
  261.8 0.7 constant_dynamic-update-slice_fusion.603
  281.1 0.7 constant_dynamic-update-slice_fusion.576
  289.0 0.7 constant_dynamic-update-slice_fusion.565
  346.9 1.1 constant_dynamic-update-slice_fusion.79
  350.8 0.7 constant_dynamic-update-slice_fusion.74
  366.5 0.7 constant_dynamic-update-slice_fusion.52
  368.1 0.9 constant_dynamic-update-slice_fusion.757
  388.5 0.7 constant_dynamic-update-slice_fusion.348
  399.2 0.9 constant_dynamic-update-slice_fusion.333
  451.4 0.7 constant_dynamic-update-slice_fusion.410
  480.6 0.7 constant_dynamic-update-slice_fusion.519
  499.9 0.7 constant_dynamic-update-slice_fusion.642
  524.2 0.7 constant_dynamic-update-slice_fusion.608
  529.2 0.7 constant_dynamic-update-slice_fusion.44
  554.2 0.7 constant_dynamic-update-slice_fusion.9
  560.8 0.7 constant_dynamic-update-slice_fusion
  561.6 9.6 %constant_dynamic-update-slice_fusion.815 = f32[32,101,512]{2,1,0:T(8,128)} fusion(bf16[512,1,6144]{2,0,1:T(8,128)(2,1)S(1)} %bitcast.1701, bf16[4,101,6144]{2,0,1:T(4,128)(2,1)} %get-tuple-element.37), kind=kOutput, calls=%fused_computation.863 | convolution fusion | flops 2541955072 | bytes 12107776 | tf_op jit(solution)/shard_map/kju,cu->kjc/dot_general | solution.py:49
  571.1 0.8 constant_dynamic-update-slice_fusion.202
  571.9 0.8 constant_dynamic-update-slice_fusion.404
  572.7 0.8 constant_dynamic-update-slice_fusion.606
  573.4 7.6 %constant_dynamic-update-slice_fusion.814 = f32[32,101,512]{2,1,0:T(8,128)} fusion(f32[32,101,512]{2,1,0:T(8,128)} %constant_dynamic-update-slice_fusion.815, bf16[512,1,6144]{2,0,1:T(8,128)(2,1)S(1)} %bitcast.1701, bf16[4,101,6144]{2,0,1:T(4,128)(2,1)S(1)} %get-tuple-element.38), kind=kOutput, calls=%fused_computation.862 | convolution fusion | flops 2541955072 | bytes 12107776 | tf_op jit(solution)/shard_map/kju,cu->kjc/dot_general | solution.py:49
  581.0 7.2 constant_dynamic-update-slice_fusion.813
  588.2 9.9 %constant_dynamic-update-slice_fusion.812 = f32[32,101,512]{2,1,0:T(8,128)} fusion(f32[32,101,512]{2,1,0:T(8,128)} %constant_dynamic-update-slice_fusion.813, bf16[512,1,6144]{2,0,1:T(8,128)(2,1)S(1)} %bitcast.1701, bf16[4,101,6144]{2,0,1:T(4,128)(2,1)} %get-tuple-element.40), kind=kOutput, calls=%fused_computation.860 | convolution fusion | flops 2541955072 | bytes 12107776 | tf_op jit(solution)/shard_map/kju,cu->kjc/dot_general | solution.py:49
  598.1 7.2 constant_dynamic-update-slice_fusion.811
  605.3 7.4 constant_dynamic-update-slice_fusion.810
  612.6 9.6 %constant_dynamic-update-slice_fusion.809 = f32[32,101,512]{2,1,0:T(8,128)} fusion(f32[32,101,512]{2,1,0:T(8,128)} %constant_dynamic-update-slice_fusion.810, bf16[512,1,6144]{2,0,1:T(8,128)(2,1)S(1)} %bitcast.1701, bf16[4,101,6144]{2,0,1:T(4,128)(2,1)} %get-tuple-element.43), kind=kOutput, calls=%fused_computation.857 | convolution fusion | flops 2541955072 | bytes 12107776 | tf_op jit(solution)/shard_map/kju,cu->kjc/dot_general | solution.py:49
  622.2 7.4 constant_dynamic-update-slice_fusion.808
  629.7 118.6 %reduce-scatter.2.cloned.1.call-done = f32[8,101,512]{2,1,0:T(8,128)} async-done(((f32[32,101,512]{2,1,0:T(8,128)}), f32[8,101,512]{2,1,0:T(8,128)}) %reduce-scatter.2.cloned.1.call-update) | async-done | bytes 1654800 | tf_op jit(solution)/shard_map/reduce_scatter | solution.py:54
  748.3 3.6 copy.12
  (820 shorter events, 460.8 us)
Async XLA Ops:
  6.5 74.0 %all-reduce.11.cloned.1.call-start = ((), (), s32[]{:S(2)}) async-start(), calls=%async_computation.2 | async-start | bytes 786432 | tf_op jit(solution)/shard_map/psum | solution.py:41
  6.5 5.9 copy-start
  23.6 724.8 %reduce-scatter.2.cloned.1.call-start = ((), (), s32[]{:S(2)}) async-start(), calls=%async_computation.1 | async-start | bytes 8519680 | tf_op jit(solution)/shard_map/reduce_scatter | solution.py:54
  245.3 122.6 %slice-start.4 = ((s8[4964352]{0:T(1024)(128)(4,1)}), s8[4194304]{0:T(1024)(128)(4,1)S(1)}, s32[]{:S(2)}) async-start(s8[4964352]{0:T(1024)(128)(4,1)} %bitcast.1704), calls=%async_computation.7 | async-start | bytes 8388608
  256.8 111.2 %slice-start.2 = ((s8[4964352]{0:T(1024)(128)(4,1)}), s8[4194304]{0:T(1024)(128)(4,1)S(1)}, s32[]{:S(2)}) async-start(s8[4964352]{0:T(1024)(128)(4,1)} %bitcast.1702), calls=%async_computation.5 | async-start | bytes 8388608
  295.4 72.6 %copy-start.1 = (bf16[4,1,6144]{2,0,1:T(4,128)(2,1)S(1)}, bf16[4,1,6144]{2,0,1:T(4,128)(2,1)}, u32[]{:S(2)}) copy-start(bf16[4,1,6144]{2,0,1:T(4,128)(2,1)} %get-tuple-element.13) | copy-start | bytes 147460
  295.4 72.6 %copy-start.2 = (bf16[4,1,6144]{2,0,1:T(4,128)(2,1)S(1)}, bf16[4,1,6144]{2,0,1:T(4,128)(2,1)}, u32[]{:S(2)}) copy-start(bf16[4,1,6144]{2,0,1:T(4,128)(2,1)} %get-tuple-element.14) | copy-start | bytes 147460
  295.4 72.6 %copy-start.3 = (bf16[4,1,6144]{2,0,1:T(4,128)(2,1)S(1)}, bf16[4,1,6144]{2,0,1:T(4,128)(2,1)}, u32[]{:S(2)}) copy-start(bf16[4,1,6144]{2,0,1:T(4,128)(2,1)} %get-tuple-element.15) | copy-start | bytes 147460
  295.4 72.6 %copy-start.4 = (bf16[4,1,6144]{2,0,1:T(4,128)(2,1)S(1)}, bf16[4,1,6144]{2,0,1:T(4,128)(2,1)}, u32[]{:S(2)}) copy-start(bf16[4,1,6144]{2,0,1:T(4,128)(2,1)} %get-tuple-element.16) | copy-start | bytes 147460
  295.4 72.6 %copy-start.5 = (bf16[4,1,6144]{2,0,1:T(4,128)(2,1)S(1)}, bf16[4,1,6144]{2,0,1:T(4,128)(2,1)}, u32[]{:S(2)}) copy-start(bf16[4,1,6144]{2,0,1:T(4,128)(2,1)} %get-tuple-element.17) | copy-start | bytes 147460
  295.4 72.6 %copy-start.6 = (bf16[4,1,6144]{2,0,1:T(4,128)(2,1)S(1)}, bf16[4,1,6144]{2,0,1:T(4,128)(2,1)}, u32[]{:S(2)}) copy-start(bf16[4,1,6144]{2,0,1:T(4,128)(2,1)} %get-tuple-element.18) | copy-start | bytes 147460
  295.5 72.6 %copy-start.7 = (bf16[4,1,6144]{2,0,1:T(4,128)(2,1)S(1)}, bf16[4,1,6144]{2,0,1:T(4,128)(2,1)}, u32[]{:S(2)}) copy-start(bf16[4,1,6144]{2,0,1:T(4,128)(2,1)} %get-tuple-element.19) | copy-start | bytes 147460
  295.5 72.6 %copy-start.8 = (bf16[4,1,6144]{2,0,1:T(4,128)(2,1)S(1)}, bf16[4,1,6144]{2,0,1:T(4,128)(2,1)}, u32[]{:S(2)}) copy-start(bf16[4,1,6144]{2,0,1:T(4,128)(2,1)} %get-tuple-element.20) | copy-start | bytes 147460
  295.5 72.6 %copy-start.9 = (bf16[4,101,6144]{2,0,1:T(4,128)(2,1)S(1)}, bf16[4,101,6144]{2,0,1:T(4,128)(2,1)}, u32[]{:S(2)}) copy-start(bf16[4,101,6144]{2,0,1:T(4,128)(2,1)} %constant_dynamic-update-slice_fusion.253) | copy-start | bytes 14893060
  306.2 61.9 %slice-start.5 = ((s8[4964352]{0:T(1024)(128)(4,1)}), s8[770048]{0:T(1024)(128)(4,1)S(1)}, s32[]{:S(2)}) async-start(s8[4964352]{0:T(1024)(128)(4,1)} %bitcast.1704), calls=%async_computation.8 | async-start | bytes 1540096
  311.9 56.2 %slice-start.3 = ((s8[4964352]{0:T(1024)(128)(4,1)}), s8[770048]{0:T(1024)(128)(4,1)S(1)}, s32[]{:S(2)}) async-start(s8[4964352]{0:T(1024)(128)(4,1)} %bitcast.1702), calls=%async_computation.6 | async-start | bytes 1540096
  443.6 118.0 %slice-start = ((s8[6291456]{0:T(1024)(128)(4,1)}), s8[4194304]{0:T(1024)(128)(4,1)S(1)}, s32[]{:S(2)}) async-start(s8[6291456]{0:T(1024)(128)(4,1)} %bitcast.1700), calls=%async_computation.3 | async-start | bytes 8388608
  502.8 58.8 %slice-start.1 = ((s8[6291456]{0:T(1024)(128)(4,1)}), s8[2097152]{0:T(1024)(128)(4,1)S(1)}, s32[]{:S(2)}) async-start(s8[6291456]{0:T(1024)(128)(4,1)} %bitcast.1700), calls=%async_computation.4 | async-start | bytes 4194304
  581.0 17.1 %slice-start.6 = ((s8[4964352]{0:T(1024)(128)(4,1)}), s8[4194304]{0:T(1024)(128)(4,1)S(1)}, s32[]{:S(2)}) async-start(s8[4964352]{0:T(1024)(128)(4,1)} %bitcast.1706), calls=%async_computation.9 | async-start | bytes 8388608
  588.2 9.9 %slice-start.7 = ((s8[4964352]{0:T(1024)(128)(4,1)}), s8[770048]{0:T(1024)(128)(4,1)S(1)}, s32[]{:S(2)}) async-start(s8[4964352]{0:T(1024)(128)(4,1)} %bitcast.1706), calls=%async_computation.10 | async-start | bytes 1540096
  588.2 17.1 %slice-start.8 = ((s8[4964352]{0:T(1024)(128)(4,1)}), s8[4194304]{0:T(1024)(128)(4,1)S(1)}, s32[]{:S(2)}) async-start(s8[4964352]{0:T(1024)(128)(4,1)} %bitcast.1708), calls=%async_computation.11 | async-start | bytes 8388608
  598.1 7.2 slice-start.9
Sparse Core Ops, SparseCore 0:
  23.7 56.7 all-reduce.10
  629.8 118.4 reduce-scatter.1
where the time goes:
time: 766 us; the launch traced here: 759 us
  local copies, waits for them, and re-layouts  484 us (63%)
  waiting for transfers between devices  175 us (23%)
  matrix products  81.5 us (11%)
  between operations  15.6 us (2%)
    unnamed x832, local copies, waits for them, and re-layouts  477 us
    reduce_scatter x1, waiting for transfers between devices, shards(): return lax.psum_scatter(stacked, 'win', scatter_dimension=0, tiled=True)  119 us
    dot_general x8, matrix products, shards(): jnp.einsum('kju,cu->kjc', shifted, traces[:, 0, :], preferred_element_typ...  65.8 us
    psum x1, waiting for transfers between devices, shards(): lax.psum(jnp.einsum('kc,cwt->kwt', select, traces, preferred_element_type...  56.1 us
    dot_general x8, matrix products, shards(): jnp.einsum('kc,cwt->kwt', select, traces, preferred_element_type=jnp.floa...  15.7 us
  transfers between devices with their start and end apart: 2, of which 2 were waited for; matrix products, arithmetic and copies ran while one was open for 0% of the time, Pallas kernels for 0%

commit v1 on v0

v1 whole, which is shorter than its diff:
```python
import functools
import math

import jax
import jax.numpy as jnp
from jax import lax
from jax.experimental import pallas as pl
from jax.experimental.pallas import tpu as pltpu
from jax.sharding import PartitionSpec as P

SAMPLES = 6000
HALF = 50
LAGS = 101
ROWS = 104
LEAD = 128
TOP = 32766.0


def code(total):
    row = lax.broadcasted_iota(jnp.int32, total.shape, 0)
    largest = jnp.max(jnp.where(row < LAGS, jnp.abs(total), 0.0), axis=0, keepdims=True)
    level = jnp.ceil(jnp.log2(jnp.maximum(largest, 1e-30)) * 16.0) + 1.0
    scaled = jnp.round(total * (jnp.exp2(level * (-1.0 / 16.0)) * TOP))
    return jnp.where(row == LAGS, level, jnp.where(row < LAGS, scaled, 0.0)).astype(jnp.int32)


def decode(coded):
    values = coded.astype(jnp.float32)
    return values * (jnp.exp2(values[LAGS : LAGS + 1] * (1.0 / 16.0)) * (1.0 / TOP))


def kernel(windows, norm_scale, depth, source_ref, trace_ref, out_ref, total, sent, landed, send_sem, recv_sem):
    place = lax.axis_index("win")
    per_group = source_ref.shape[0] // (2 * windows)
    span_len = trace_ref.shape[0]

    barrier = pltpu.get_barrier_semaphore()

    @pl.when(place > 0)
    def _():
        pl.semaphore_signal(barrier, inc=1, device_id={"win": place - 1}, device_id_type=pl.DeviceIdType.MESH)

    @pl.when(place < windows - 1)
    def _():
        pl.semaphore_signal(barrier, inc=1, device_id={"win": place + 1}, device_id_type=pl.DeviceIdType.MESH)

    pl.semaphore_wait(barrier, jnp.where(place > 0, 1, 0) + jnp.where(place < windows - 1, 1, 0))

    def correlate(pair):
        total[...] = jnp.zeros_like(total)

        @pl.loop(0, span_len // depth)
        def _(piece):
            begin = pl.multiple_of(piece * depth, depth)
            lags = []
            for member in range(2):
                record = source_ref[pl.ds(2 * pair + member, 1), pl.ds(begin, LEAD + depth)]
                spread = jnp.broadcast_to(record, (ROWS, LEAD + depth))
                lags.append(pltpu.roll(spread, 0, 1, stride=1, stride_axis=0)[:, LEAD:])
            shifted = jnp.concatenate(lags, axis=0).astype(jnp.bfloat16)
            total[...] += jnp.dot(shifted, trace_ref[pl.ds(begin, depth), :], preferred_element_type=jnp.float32)

        total[...] *= norm_scale

    def landing(way, pair):
        return pltpu.make_async_remote_copy(
            src_ref=sent.at[pair],
            dst_ref=landed.at[way, pair],
            send_sem=send_sem.at[pair],
            recv_sem=recv_sem.at[way, pair],
            device_id={"win": place + 1 - 2 * way},
            device_id_type=pl.DeviceIdType.MESH,
        )

    def add_landed(way, pair):
        landing(way, pair).wait_recv()
        for member in range(2):
            rows = slice(member * ROWS, (member + 1) * ROWS)
            total[rows] += decode(landed[way, pair].astype(jnp.int32)[rows])

    @pl.loop(0, 2 * (windows - 1) * per_group)
    def _(slot):
        stage = slot // (2 * per_group)
        inner = lax.rem(slot // 2, per_group)
        way = lax.rem(slot, 2)
        group = jnp.where(way == 0, windows - 1 - stage, stage)
        active = jnp.where(way == 0, group > place, group < place)

        @pl.when(active)
        def _():
            pair = group * per_group + inner
            correlate(pair)

            @pl.when(jnp.where(way == 0, place > 0, place < windows - 1))
            def _():
                add_landed(way, pair)

            coded = [code(total[member * ROWS : (member + 1) * ROWS]) for member in range(2)]
            sent[pair] = jnp.concatenate(coded, axis=0).astype(jnp.int16)
            landing(way, pair).start()

    @pl.loop(0, per_group)
    def _(inner):
        pair = place * per_group + inner
        correlate(pair)

        @pl.when(place > 0)
        def _():
            add_landed(0, pair)

        @pl.when(place < windows - 1)
        def _():
            add_landed(1, pair)

        for member in range(2):
            out_ref[2 * inner + member] = total[member * ROWS : member * ROWS + LAGS]

    @pl.loop(0, windows * per_group)
    def _(pair):
        @pl.when(pair // per_group != place)
        def _():
            landing(0, pair).wait_send()


def shards(traces, sources, offsets):
    ch_dev = traces.shape[0]
    span_len = traces.shape[2]
    source_count = sources.size
    windows = lax.axis_size("win")
    first_row = lax.axis_index("rcv") * ch_dev
    norm_scale = 1.0 / math.sqrt(SAMPLES * windows * traces.shape[1])
    local = traces[:, 0, :]
    wanted = sources.reshape(-1) - first_row
    select = (wanted[:, None] == jnp.arange(ch_dev, dtype=jnp.int32)[None, :]).astype(traces.dtype)
    picked = jnp.dot(select, local, preferred_element_type=jnp.float32).astype(traces.dtype)
    records = lax.psum(picked, "rcv")
    positions = jnp.arange(span_len, dtype=jnp.int32)
    start_at = offsets[0] + HALF
    inside = (positions >= start_at) & (positions < start_at + SAMPLES)
    masked = jnp.where(inside[None, :], records.astype(jnp.float32), 0.0)
    padded = jnp.pad(masked, ((0, 0), (LEAD - HALF, HALF)))
    pairs = source_count // 2
    group = source_count // windows
    return pl.pallas_call(
        functools.partial(kernel, windows, norm_scale, 512),
        out_shape=jax.ShapeDtypeStruct((group, LAGS, ch_dev), jnp.float32),
        in_specs=[pl.BlockSpec(memory_space=pltpu.VMEM)] * 2,
        out_specs=pl.BlockSpec(memory_space=pltpu.VMEM),
        scratch_shapes=[
            pltpu.VMEM((2 * ROWS, ch_dev), jnp.float32),
            pltpu.VMEM((pairs, 2 * ROWS, ch_dev), jnp.int16),
            pltpu.VMEM((2, pairs, 2 * ROWS, ch_dev), jnp.int16),
            pltpu.SemaphoreType.DMA((pairs,)),
            pltpu.SemaphoreType.DMA((2, pairs)),
        ],
        compiler_params=pltpu.CompilerParams(
            collective_id=0, has_side_effects=True, vmem_limit_bytes=56 * 1024 * 1024
        ),
        cost_estimate=pl.CostEstimate(
            flops=2 * source_count * ROWS * ch_dev * span_len,
            bytes_accessed=2 * ch_dev * span_len,
            transcendentals=0,
        ),
    )(padded, local.T)


def solution(mesh):
    in_specs = (P("rcv", "win", None), P(), P("win"))
    out_specs = P("win", None, "rcv")
    return jax.shard_map(shards, mesh=mesh, in_specs=in_specs, out_specs=out_specs, check_vma=False)
```

time: 766 us -> 200 us (0.26)
  local copies, waits for them, and re-layouts: 484 us -> 13.6 us
  waiting for transfers between devices: 175 us -> 46 us
  Pallas kernels: 0 us -> 120 us
  matrix products: 81.5 us -> 4.73 us
    unnamed x832 -> x1, local copies, waits for them, and re-layouts: 477 us -> 8.72 us
    pallas_call x0 -> x1, Pallas kernels: none -> 120 us  [shards(): pl.pallas_call(functools.partial(kernel, windows, norm_scale, 512), out_s...]
    reduce_scatter x1 -> x0, waiting for transfers between devices: 119 us -> none  [shards(): return lax.psum_scatter(stacked, 'win', scatter_dimension=0, tiled=True)]
    dot_general x16 -> x1, matrix products: 81.5 us -> 4.73 us  [shards(): jnp.dot(select, local, preferred_element_type=jnp.float32)]
    psum x1, waiting for transfers between devices: 56.1 us -> 46 us  [shards(): records = lax.psum(picked, 'rcv')]
  transfers between devices with their start and end apart: 2 -> 1, of which waited for: 2 -> 1; matrix products, arithmetic and copies ran while one was open for 0% -> 4% of each run, Pallas kernels for 0% -> 0%
where the time goes in v1:
time: 200 us
  Pallas kernels  120 us (60%)
  waiting for transfers between devices  46 us (23%)
  between operations  14.1 us (7%)
  local copies, waits for them, and re-layouts  13.6 us (7%)
  matrix products  4.73 us (2%)
    pallas_call x1, Pallas kernels, shards(): pl.pallas_call(functools.partial(kernel, windows, norm_scale, 512), out_s...  120 us
    psum x1, waiting for transfers between devices, shards(): records = lax.psum(picked, 'rcv')  46 us
    unnamed x1, local copies, waits for them, and re-layouts  8.72 us
    dot_general x1, matrix products, shards(): jnp.dot(select, local, preferred_element_type=jnp.float32)  4.73 us
  transfers between devices with their start and end apart: 1, of which 1 were waited for; matrix products, arithmetic and copies ran while one was open for 4% of the time, Pallas kernels for 0%

profile of v1, /device:TPU:8, one launch (start us, length us, event | category | flops | bytes accessed | tf_op | source)
XLA Modules:
  0.0 199.7 jit_solution(16113646195084165546)
XLA Ops:
  6.5 0.0 all-reduce.3.cloned.1.call-start
  6.5 0.7 broadcast_subtract_fusion
  7.2 0.1 copy.7
  7.3 0.1 sub.15
  7.4 4.7 %convolution_convert_fusion = bf16[32,6144]{1,0:T(8,128)(2,1)} fusion(bf16[512,1,6144]{2,0,1:T(8,128)(2,1)} %param.3, s32[32]{0:T(128)S(1)} %sub.15), kind=kOutput, calls=%fused_computation | convolution fusion | flops 201539584 | bytes 6684800 | tf_op jit(solution)/shard_map/dot_general | solution.py:135
  12.1 0.0 all-reduce.3.cloned.1.call-update
  12.1 8.7 %copy.8 = bf16[512,1,6144]{0,2,1:T(8,128)(2,1)} copy(bf16[512,1,6144]{2,0,1:T(8,128)(2,1)} %param.3) | data formatting | bytes 12582912 | tf_op args[0]
  21.5 46.0 %all-reduce.3.cloned.1.call-done = bf16[32,6144]{1,0:T(8,128)(2,1)} async-done(((bf16[32,6144]{1,0:T(8,128)(2,1)}), bf16[32,6144]{1,0:T(8,128)(2,1)}) %all-reduce.3.cloned.1.call-update) | async-done | bytes 393232 | tf_op jit(solution)/shard_map/psum | solution.py:136
  67.5 1.1 convert_select_fusion
  68.6 1.2 pad.4.source_ref
  69.7 119.6 %shard_map.37 = f32[8,101,512]{2,1,0:T(8,128)} custom-call(f32[32,6272]{1,0:T(8,128)} %pad.4.source_ref, bf16[6144,512]{1,0:T(8,128)(2,1)} %bitcast.8), custom_call_target="tpu_custom_call" | custom-call | flops 20937965568 | bytes 6291456 | tf_op jit(solution)/shard_map/pallas_call | solution.py:144
  189.3 3.6 %copy.9 = f32[8,101,512]{2,0,1:T(8,128)} copy(f32[8,101,512]{2,1,0:T(8,128)} %shard_map.37) | data formatting | bytes 3309568 | tf_op jit(solution)/shard_map/pallas_call | solution.py:144
  (1 shorter events, 0.0 us)
Async XLA Ops:
  6.5 61.0 %all-reduce.3.cloned.1.call-start = ((), (), s32[]{:S(2)}) async-start(), calls=%async_computation | async-start | bytes 786432 | tf_op jit(solution)/shard_map/psum | solution.py:136
Sparse Core Ops, SparseCore 0:
  12.3 55.1 all-reduce.2

commit v2 on v1

v2 whole, which is shorter than its diff:
```python
import functools
import math

import jax
import jax.numpy as jnp
from jax import lax
from jax.experimental import pallas as pl
from jax.experimental.pallas import tpu as pltpu
from jax.sharding import PartitionSpec as P

SAMPLES = 6000
HALF = 50
LAGS = 101
ROWS = 104
LEAD = 128
FOLD = 16
TOP = 32766.0


def code(total):
    row = lax.broadcasted_iota(jnp.int32, total.shape, 0)
    largest = jnp.max(jnp.where(row < LAGS, jnp.abs(total), 0.0), axis=0, keepdims=True)
    level = jnp.ceil(jnp.log2(jnp.maximum(largest, 1e-30)) * 16.0) + 1.0
    scaled = jnp.round(total * (jnp.exp2(level * (-1.0 / 16.0)) * TOP))
    return jnp.where(row == LAGS, level, jnp.where(row < LAGS, scaled, 0.0)).astype(jnp.int32)


def decode(coded):
    values = coded.astype(jnp.float32)
    return values * (jnp.exp2(values[LAGS : LAGS + 1] * (1.0 / 16.0)) * (1.0 / TOP))


def kernel(parts, windows, norm_scale, members, depth, source_ids, offset_ref, trace_hbm, out_ref,
           trace, packed, met, found, rows, padded, total, sent, landed,
           load_sem, meet_send, meet_recv, find_send, find_recv, send_sem, recv_sem):
    place = lax.axis_index("win")
    own = lax.axis_index("rcv")
    ch_dev, span_len = trace.shape
    source_count = rows.shape[0]
    per_part = source_count // parts
    slabs = FOLD // per_part
    width = span_len // slabs
    quads = source_count // (members * windows)
    last = windows - 1

    def load(slab):
        columns = pl.ds(slab * width, width)
        return pltpu.make_async_copy(trace_hbm.at[:, columns], trace.at[:, columns], load_sem.at[slab])

    for slab in range(slabs):
        load(slab).start()

    def greet(coordinates):
        pl.semaphore_signal(barrier, inc=1, device_id=coordinates, device_id_type=pl.DeviceIdType.MESH)

    barrier = pltpu.get_barrier_semaphore()
    for hop in range(1, parts):
        greet({"rcv": lax.rem(own + hop, parts)})

    @pl.when(place > 0)
    def _():
        greet({"win": place - 1})

    @pl.when(place < last)
    def _():
        greet({"win": place + 1})

    row = lax.broadcasted_iota(jnp.int32, (parts * FOLD, ch_dev), 0)
    channel = lax.broadcasted_iota(jnp.int32, (parts * FOLD, ch_dev), 1) + own * ch_dev
    source_of = (row // FOLD) * per_part + lax.rem(row, per_part)
    slab_of = lax.rem(row, FOLD) // per_part
    wanted = jnp.zeros(row.shape, jnp.int32)
    group_size = source_count // source_ids.shape[0]
    for source in range(source_count):
        wanted = jnp.where(source_of == source, source_ids[source // group_size, source % group_size], wanted)
    picked = jnp.zeros((parts * FOLD, width), jnp.float32)
    for slab in range(slabs):
        load(slab).wait()
        select = jnp.where((wanted == channel) & (slab_of == slab), 1.0, 0.0).astype(trace.dtype)
        picked += jnp.dot(select, trace[:, slab * width : (slab + 1) * width], preferred_element_type=jnp.float32)
    packed[...] = picked.astype(packed.dtype).reshape(packed.shape)

    pl.semaphore_wait(barrier, parts - 1 + jnp.where(place > 0, 1, 0) + jnp.where(place < last, 1, 0))

    def meet(hop):
        peer = lax.rem(own + hop, parts)
        return pltpu.make_async_remote_copy(
            src_ref=packed.at[peer], dst_ref=met.at[hop - 1], send_sem=meet_send.at[hop - 1],
            recv_sem=meet_recv.at[hop - 1], device_id={"rcv": peer}, device_id_type=pl.DeviceIdType.MESH)

    def find(hop):
        peer = lax.rem(own + hop, parts)
        return pltpu.make_async_remote_copy(
            src_ref=found.at[own], dst_ref=found.at[own], send_sem=find_send.at[hop - 1],
            recv_sem=find_recv.at[hop - 1], device_id={"rcv": peer}, device_id_type=pl.DeviceIdType.MESH)

    for hop in range(1, parts):
        meet(hop).start()
    record = packed[own].astype(jnp.float32)
    for hop in range(1, parts):
        meet(hop).wait_recv()
        record += met[hop - 1].astype(jnp.float32)
    found[own] = record.astype(found.dtype)
    for hop in range(1, parts):
        find(hop).start()
    for hop in range(1, parts):
        find(hop).wait_recv()
    for part in range(parts):
        block = found[part].astype(jnp.float32)
        for slab in range(slabs):
            rows[part * per_part : (part + 1) * per_part, slab * width : (slab + 1) * width] = block[
                slab * per_part : (slab + 1) * per_part
            ]
    position = lax.broadcasted_iota(jnp.int32, rows.shape, 1)
    start_at = offset_ref[0] + HALF
    masked = jnp.where((position >= start_at) & (position < start_at + SAMPLES), rows[...], 0.0)
    padded[...] = pltpu.roll(
        jnp.concatenate([masked, jnp.zeros((source_count, LEAD), jnp.float32)], axis=1), LEAD - HALF, 1
    )

    def correlate(quad):
        total[...] = jnp.zeros_like(total)

        @pl.loop(0, span_len // depth)
        def _(piece):
            begin = pl.multiple_of(piece * depth, depth)
            lags = []
            for member in range(members):
                line = padded[pl.ds(members * quad + member, 1), pl.ds(begin, LEAD + depth)]
                spread = jnp.broadcast_to(line, (ROWS, LEAD + depth))
                lags.append(pltpu.roll(spread, 0, 1, stride=1, stride_axis=0)[:, LEAD:])
            shifted = jnp.concatenate(lags, axis=0).astype(jnp.bfloat16)
            total[...] += lax.dot_general(
                shifted, trace[:, pl.ds(begin, depth)], (((1,), (1,)), ((), ())), preferred_element_type=jnp.float32
            )

        total[...] *= norm_scale

    pairs_in = members // 2

    def landing(way, pair):
        return pltpu.make_async_remote_copy(
            src_ref=sent.at[pair],
            dst_ref=landed.at[way, pair],
            send_sem=send_sem.at[pair],
            recv_sem=recv_sem.at[way, pair],
            device_id={"win": place + 1 - 2 * way},
            device_id_type=pl.DeviceIdType.MESH,
        )

    def add_landed(way, pair, base):
        landing(way, pair).wait_recv()
        coded = landed[way, pair].astype(jnp.int32)
        for member in range(2):
            total[base + member * ROWS : base + (member + 1) * ROWS] += decode(coded[member * ROWS : (member + 1) * ROWS])

    @pl.loop(0, 2 * last * quads)
    def _(slot):
        stage = slot // (2 * quads)
        inner = lax.rem(slot // 2, quads)
        way = lax.rem(slot, 2)
        group = jnp.where(way == 0, last - stage, stage)

        @pl.when(jnp.where(way == 0, group > place, group < place))
        def _():
            quad = group * quads + inner
            correlate(quad)
            for half in range(pairs_in):
                pair = quad * pairs_in + half
                base = half * 2 * ROWS

                @pl.when(jnp.where(way == 0, place > 0, place < last))
                def _():
                    add_landed(way, pair, base)

                coded = [code(total[base + member * ROWS : base + (member + 1) * ROWS]) for member in range(2)]
                sent[pair] = jnp.concatenate(coded, axis=0).astype(jnp.int16)
                landing(way, pair).start()

    @pl.loop(0, quads)
    def _(inner):
        quad = place * quads + inner
        correlate(quad)
        for half in range(pairs_in):
            pair = quad * pairs_in + half
            base = half * 2 * ROWS

            @pl.when(place > 0)
            def _():
                add_landed(0, pair, base)

            @pl.when(place < last)
            def _():
                add_landed(1, pair, base)

        for member in range(members):
            out_ref[members * inner + member] = total[member * ROWS : member * ROWS + LAGS]

    for hop in range(1, parts):
        meet(hop).wait_send()
        find(hop).wait_send()

    @pl.loop(0, source_count // 2)
    def _(pair):
        @pl.when(pair // (quads * pairs_in) != place)
        def _():
            landing(0, pair).wait_send()


def shards(traces, sources, offsets):
    ch_dev, win_dev, span_len = traces.shape
    source_count = sources.size
    windows = lax.axis_size("win")
    parts = lax.axis_size("rcv")
    norm_scale = 1.0 / math.sqrt(SAMPLES * windows * win_dev)
    members = 4
    slabs = FOLD * parts // source_count
    width = span_len // slabs
    pairs = source_count // 2
    group = source_count // windows
    return pl.pallas_call(
        functools.partial(kernel, parts, windows, norm_scale, members, 2048),
        out_shape=jax.ShapeDtypeStruct((group, LAGS, ch_dev), jnp.float32),
        in_specs=[
            pl.BlockSpec(memory_space=pltpu.SMEM),
            pl.BlockSpec(memory_space=pltpu.SMEM),
            pl.BlockSpec(memory_space=pl.ANY),
        ],
        out_specs=pl.BlockSpec(memory_space=pltpu.VMEM),
        scratch_shapes=[
            pltpu.VMEM((ch_dev, span_len), traces.dtype),
            pltpu.VMEM((parts, FOLD, width), traces.dtype),
            pltpu.VMEM((parts - 1, FOLD, width), traces.dtype),
            pltpu.VMEM((parts, FOLD, width), traces.dtype),
            pltpu.VMEM((source_count, span_len), jnp.float32),
            pltpu.VMEM((source_count, span_len + LEAD), jnp.float32),
            pltpu.VMEM((members * ROWS, ch_dev), jnp.float32),
            pltpu.VMEM((pairs, 2 * ROWS, ch_dev), jnp.int16),
            pltpu.VMEM((2, pairs, 2 * ROWS, ch_dev), jnp.int16),
            pltpu.SemaphoreType.DMA((slabs,)),
            pltpu.SemaphoreType.DMA((parts - 1,)),
            pltpu.SemaphoreType.DMA((parts - 1,)),
            pltpu.SemaphoreType.DMA((parts - 1,)),
            pltpu.SemaphoreType.DMA((parts - 1,)),
            pltpu.SemaphoreType.DMA((pairs,)),
            pltpu.SemaphoreType.DMA((2, pairs)),
        ],
        compiler_params=pltpu.CompilerParams(
            collective_id=0, has_side_effects=True, vmem_limit_bytes=56 * 1024 * 1024
        ),
        cost_estimate=pl.CostEstimate(
            flops=2 * source_count * ROWS * ch_dev * span_len,
            bytes_accessed=2 * ch_dev * span_len,
            transcendentals=0,
        ),
    )(sources, offsets, traces.reshape(ch_dev, span_len))


def solution(mesh):
    in_specs = (P("rcv", "win", None), P(), P("win"))
    out_specs = P("win", None, "rcv")
    return jax.shard_map(shards, mesh=mesh, in_specs=in_specs, out_specs=out_specs, check_vma=False)
```

time: 200 us -> 107 us (0.54)
  waiting for transfers between devices: 46 us -> 0 us
  Pallas kernels: 120 us -> 100 us
  between operations: 14.1 us -> 0.66 us
  local copies, waits for them, and re-layouts: 13.6 us -> 4.93 us
  matrix products: 4.73 us -> 0 us
    psum x1 -> x0, waiting for transfers between devices: 46 us -> none  [shards(): records = lax.psum(picked, 'rcv')]
    pallas_call x1, Pallas kernels: 120 us -> 100 us  [shards(): pl.pallas_call(functools.partial(kernel, parts, windows, norm_scale, memb...]
    unnamed x1, local copies, waits for them, and re-layouts: 8.72 us -> 1.35 us
    dot_general x1 -> x0, matrix products: 4.73 us -> none  [shards(): jnp.dot(select, local, preferred_element_type=jnp.float32)]
  transfers between devices with their start and end apart: 1 -> 0, of which waited for: 1 -> 0; matrix products, arithmetic and copies ran while one was open for 4% -> 0% of each run, Pallas kernels for 0% -> 0%
where the time goes in v2:
time: 107 us; the launch traced here: 106 us
  Pallas kernels  100 us (93%)
  local copies, waits for them, and re-layouts  4.93 us (5%)
    pallas_call x1, Pallas kernels, shards(): pl.pallas_call(functools.partial(kernel, parts, windows, norm_scale, memb...  100 us
    pallas_call x1, local copies, waits for them, and re-layouts, shards(): pl.pallas_call(functools.partial(kernel, parts, windows, norm_scale, memb...  3.58 us

profile of v2, /device:TPU:8, one launch (start us, length us, event | category | flops | bytes accessed | tf_op | source)
XLA Modules:
  0.0 105.8 jit_solution(10719654831029390188)
XLA Ops:
  0.7 1.3 %copy.4.source_ids = s32[8,4]{1,0:T(8,128)} copy(s32[8,4]{0,1:T(4,128)} %param.4) | data formatting | bytes 256 | tf_op args[1]
  2.0 100.2 %shard_map.37 = f32[8,101,512]{2,1,0:T(8,128)} custom-call(s32[8,4]{1,0:T(8,128)} %copy.4.source_ids, s32[1]{0:T(128)S(6)} %copy.6.offset_ref, bf16[512,6144]{1,0:T(8,128)(2,1)} %bitcast.1), custom_call_target="tpu_custom_call" | custom-call | flops 20937965568 | bytes 6291456 | tf_op jit(solution)/shard_map/pallas_call | solution.py:221
  102.2 3.6 %copy.5 = f32[8,101,512]{2,0,1:T(8,128)} copy(f32[8,101,512]{2,1,0:T(8,128)} %shard_map.37) | data formatting | bytes 3309568 | tf_op jit(solution)/shard_map/pallas_call | solution.py:221

commit v3 on v2

--- a/solution.py
+++ b/solution.py
@@ -14,6 +14,7 @@
 ROWS = 104
 LEAD = 128
 FOLD = 16
+AHEAD = 2
 TOP = 32766.0
 
 
@@ -70,9 +71,9 @@
     source_of = (row // FOLD) * per_part + lax.rem(row, per_part)
     slab_of = lax.rem(row, FOLD) // per_part
     wanted = jnp.zeros(row.shape, jnp.int32)
-    group_size = source_count // source_ids.shape[0]
+    group_size = source_ids.shape[0]
     for source in range(source_count):
-        wanted = jnp.where(source_of == source, source_ids[source // group_size, source % group_size], wanted)
+        wanted = jnp.where(source_of == source, source_ids[source % group_size, source // group_size], wanted)
     picked = jnp.zeros((parts * FOLD, width), jnp.float32)
     for slab in range(slabs):
         load(slab).wait()
@@ -118,8 +119,8 @@
         jnp.concatenate([masked, jnp.zeros((source_count, LEAD), jnp.float32)], axis=1), LEAD - HALF, 1
     )
 
-    def correlate(quad):
-        total[...] = jnp.zeros_like(total)
+    def correlate(quad, slot):
+        total[slot] = jnp.zeros(total.shape[1:], total.dtype)
 
         @pl.loop(0, span_len // depth)
         def _(piece):
@@ -130,13 +131,14 @@
                 spread = jnp.broadcast_to(line, (ROWS, LEAD + depth))
                 lags.append(pltpu.roll(spread, 0, 1, stride=1, stride_axis=0)[:, LEAD:])
             shifted = jnp.concatenate(lags, axis=0).astype(jnp.bfloat16)
-            total[...] += lax.dot_general(
+            total[slot] += lax.dot_general(
                 shifted, trace[:, pl.ds(begin, depth)], (((1,), (1,)), ((), ())), preferred_element_type=jnp.float32
             )
 
-        total[...] *= norm_scale
+        total[slot] *= norm_scale
 
     pairs_in = members // 2
+    per_group = quads * pairs_in
 
     def landing(way, pair):
         return pltpu.make_async_remote_copy(
@@ -148,63 +150,90 @@
             device_id_type=pl.DeviceIdType.MESH,
         )
 
-    def add_landed(way, pair, base):
+    def add_landed(way, pair, slot, base):
         landing(way, pair).wait_recv()
         coded = landed[way, pair].astype(jnp.int32)
         for member in range(2):
-            total[base + member * ROWS : base + (member + 1) * ROWS] += decode(coded[member * ROWS : (member + 1) * ROWS])
+            part_rows = slice(base + member * ROWS, base + (member + 1) * ROWS)
+            total[slot, part_rows] += decode(coded[member * ROWS : (member + 1) * ROWS])
+
+    def pair_at(way, turn):
+        group = jnp.where(way == 0, last - turn // per_group, turn // per_group)
+        return group * per_group + lax.rem(turn, per_group)
+
+    between = (place > 0) & (place < last)
+    first_way = jnp.where(2 * place < windows, 0, 1)
+
+    @pl.when(between)
+    def _():
+        @pl.loop(0, quads)
+        def _(inner):
+            correlate(place * quads + inner, inner)
 
     @pl.loop(0, 2 * last * quads)
     def _(slot):
         stage = slot // (2 * quads)
         inner = lax.rem(slot // 2, quads)
-        way = lax.rem(slot, 2)
+        way = lax.rem(slot + first_way, 2)
         group = jnp.where(way == 0, last - stage, stage)
 
         @pl.when(jnp.where(way == 0, group > place, group < place))
         def _():
             quad = group * quads + inner
-            correlate(quad)
+            correlate(quad, quads)
             for half in range(pairs_in):
                 pair = quad * pairs_in + half
+                turn = (stage * quads + inner) * pairs_in + half
                 base = half * 2 * ROWS
 
                 @pl.when(jnp.where(way == 0, place > 0, place < last))
                 def _():
-                    add_landed(way, pair, base)
-
-                coded = [code(total[base + member * ROWS : base + (member + 1) * ROWS]) for member in range(2)]
+                    add_landed(way, pair, quads, base)
+
+                coded = [code(total[quads, base + member * ROWS : base + (member + 1) * ROWS]) for member in range(2)]
                 sent[pair] = jnp.concatenate(coded, axis=0).astype(jnp.int16)
+
+                @pl.when(turn >= AHEAD)
+                def _():
+                    landing(way, pair_at(way, turn - AHEAD)).wait_send()
+
                 landing(way, pair).start()
+
+    @pl.when(jnp.logical_not(between))
+    def _():
+        @pl.loop(0, quads)
+        def _(inner):
+            correlate(place * quads + inner, inner)
 
     @pl.loop(0, quads)
     def _(inner):
-        quad = place * quads + inner
-        correlate(quad)
         for half in range(pairs_in):
-            pair = quad * pairs_in + half
+            pair = (place * quads + inner) * pairs_in + half
             base = half * 2 * ROWS
 
             @pl.when(place > 0)
             def _():
-                add_landed(0, pair, base)
+                add_landed(0, pair, inner, base)
 
             @pl.when(place < last)
             def _():
-                add_landed(1, pair, base)
+                add_landed(1, pair, inner, base)
 
         for member in range(members):
-            out_ref[members * inner + member] = total[member * ROWS : member * ROWS + LAGS]
+            out_ref[members * inner + member] = total[inner, member * ROWS : member * ROWS + LAGS]
 
     for hop in range(1, parts):
         meet(hop).wait_send()
         find(hop).wait_send()
 
-    @pl.loop(0, source_count // 2)
-    def _(pair):
-        @pl.when(pair // (quads * pairs_in) != place)
-        def _():
-            landing(0, pair).wait_send()
+    for way in range(2):
+        turns = (place if way else last - place) * per_group
+
+        @pl.loop(0, last * per_group)
+        def _(turn):
+            @pl.when((turn < turns) & (turn >= turns - AHEAD))
+            def _():
+                landing(way, pair_at(way, turn)).wait_send()
 
 
 def shards(traces, sources, offsets):
@@ -234,7 +263,7 @@
             pltpu.VMEM((parts, FOLD, width), traces.dtype),
             pltpu.VMEM((source_count, span_len), jnp.float32),
             pltpu.VMEM((source_count, span_len + LEAD), jnp.float32),
-            pltpu.VMEM((members * ROWS, ch_dev), jnp.float32),
+            pltpu.VMEM((group // members + 1, members * ROWS, ch_dev), jnp.float32),
             pltpu.VMEM((pairs, 2 * ROWS, ch_dev), jnp.int16),
             pltpu.VMEM((2, pairs, 2 * ROWS, ch_dev), jnp.int16),
             pltpu.SemaphoreType.DMA((slabs,)),
@@ -253,7 +282,7 @@
             bytes_accessed=2 * ch_dev * span_len,
             transcendentals=0,
         ),
-    )(sources, offsets, traces.reshape(ch_dev, span_len))
+    )(sources.T, offsets, traces.reshape(ch_dev, span_len))
 
 
 def solution(mesh):

time: 107 us -> 84.7 us (0.79)
  Pallas kernels: 100 us -> 79 us
  local copies, waits for them, and re-layouts: 4.93 us -> 3.58 us
    pallas_call x1, Pallas kernels: 100 us -> 79 us  [shards(): pl.pallas_call(functools.partial(kernel, parts, windows, norm_scale, memb...]
    unnamed x1 -> x0, local copies, waits for them, and re-layouts: 1.35 us -> none
where the time goes in v3:
time: 84.7 us; the launch traced here: 83.3 us
  Pallas kernels  79 us (93%)
  local copies, waits for them, and re-layouts  3.58 us (4%)
    pallas_call x1, Pallas kernels, shards(): pl.pallas_call(functools.partial(kernel, parts, windows, norm_scale, memb...  79 us
    pallas_call x1, local copies, waits for them, and re-layouts, shards(): pl.pallas_call(functools.partial(kernel, parts, windows, norm_scale, memb...  3.58 us

profile of v3, /device:TPU:8, one launch (start us, length us, event | category | flops | bytes accessed | tf_op | source)
XLA Modules:
  0.0 83.3 jit_solution(13939469334600063906)
XLA Ops:
  0.7 79.0 %shard_map.37 = f32[8,101,512]{2,1,0:T(8,128)} custom-call(s32[4,8]{1,0:T(4,128)} %bitcast.3, s32[1]{0:T(128)S(6)} %copy.5.offset_ref, bf16[512,6144]{1,0:T(8,128)(2,1)} %bitcast.2), custom_call_target="tpu_custom_call" | custom-call | flops 20937965568 | bytes 6291456 | tf_op jit(solution)/shard_map/pallas_call | solution.py:250
  79.7 3.6 %copy.4 = f32[8,101,512]{2,0,1:T(8,128)} copy(f32[8,101,512]{2,1,0:T(8,128)} %shard_map.37) | data formatting | bytes 3309568 | tf_op jit(solution)/shard_map/pallas_call | solution.py:250

commit v4 on v3

--- a/solution.py
+++ b/solution.py
@@ -119,23 +119,24 @@
         jnp.concatenate([masked, jnp.zeros((source_count, LEAD), jnp.float32)], axis=1), LEAD - HALF, 1
     )
 
-    def correlate(quad, slot):
-        total[slot] = jnp.zeros(total.shape[1:], total.dtype)
+    def correlate(quad, slot, least=0, count=members):
+        block = slice(least * ROWS, (least + count) * ROWS)
+        total[slot, block] = jnp.zeros((count * ROWS, ch_dev), total.dtype)
 
         @pl.loop(0, span_len // depth)
         def _(piece):
             begin = pl.multiple_of(piece * depth, depth)
             lags = []
-            for member in range(members):
+            for member in range(least, least + count):
                 line = padded[pl.ds(members * quad + member, 1), pl.ds(begin, LEAD + depth)]
                 spread = jnp.broadcast_to(line, (ROWS, LEAD + depth))
                 lags.append(pltpu.roll(spread, 0, 1, stride=1, stride_axis=0)[:, LEAD:])
             shifted = jnp.concatenate(lags, axis=0).astype(jnp.bfloat16)
-            total[slot] += lax.dot_general(
+            total[slot, block] += lax.dot_general(
                 shifted, trace[:, pl.ds(begin, depth)], (((1,), (1,)), ((), ())), preferred_element_type=jnp.float32
             )
 
-        total[slot] *= norm_scale
+        total[slot, block] *= norm_scale
 
     pairs_in = members // 2
     per_group = quads * pairs_in
@@ -180,8 +181,18 @@
         @pl.when(jnp.where(way == 0, group > place, group < place))
         def _():
             quad = group * quads + inner
-            correlate(quad, quads)
+            opening = (stage == 0) & (inner == 0)
+
+            @pl.when(jnp.logical_not(opening))
+            def _():
+                correlate(quad, quads)
+
             for half in range(pairs_in):
+
+                @pl.when(opening)
+                def _():
+                    correlate(quad, quads, 2 * half, 2)
+
                 pair = quad * pairs_in + half
                 turn = (stage * quads + inner) * pairs_in + half
                 base = half * 2 * ROWS

time: 84.7 us -> 83.9 us (level)
  no operation moved by 1% of the time
where the time goes in v4:
time: 83.9 us; the launch traced here: 82.4 us
  Pallas kernels  78.2 us (93%)
  local copies, waits for them, and re-layouts  3.58 us (4%)
    pallas_call x1, Pallas kernels, shards(): pl.pallas_call(functools.partial(kernel, parts, windows, norm_scale, memb...  78.2 us
    pallas_call x1, local copies, waits for them, and re-layouts, shards(): pl.pallas_call(functools.partial(kernel, parts, windows, norm_scale, memb...  3.58 us

profile of v4, /device:TPU:8, one launch (start us, length us, event | category | flops | bytes accessed | tf_op | source)
XLA Modules:
  0.0 82.4 jit_solution(15398892446754441381)
XLA Ops:
  0.7 78.2 %shard_map.37 = f32[8,101,512]{2,1,0:T(8,128)} custom-call(s32[4,8]{1,0:T(4,128)} %bitcast.3, s32[1]{0:T(128)S(6)} %copy.5.offset_ref, bf16[512,6144]{1,0:T(8,128)(2,1)} %bitcast.2), custom_call_target="tpu_custom_call" | custom-call | flops 20937965568 | bytes 6291456 | tf_op jit(solution)/shard_map/pallas_call | solution.py:261
  78.9 3.6 %copy.4 = f32[8,101,512]{2,0,1:T(8,128)} copy(f32[8,101,512]{2,1,0:T(8,128)} %shard_map.37) | data formatting | bytes 3309568 | tf_op jit(solution)/shard_map/pallas_call | solution.py:261
